TPU v7x, 32 devices: a whole 2x2x4 slice. The times are simulated.
32 devices in a mesh: groups: 2 (over y), expert: 16 (over z, x, core).
Axes of the slice: x: 2, y: 2, z: 4, core: 2. Of those that a mesh axis runs over, the one named last changes fastest.
Arguments:
- tokens: bfloat16 [4096, 3584], P(('groups', 'expert')), parts along dimension 0, may hold values from -6 to 6
- routes: int32 [4096, 2], P(('groups', 'expert')), parts along dimension 0, may hold values from 0 to 3, all different within a row; in each aligned block of 128 rows (0 to 127, 128 to 255, ...) at most 96 rows name the same one
- gates: float32 [4096, 2], P(('groups', 'expert')), parts along dimension 0, may hold values from 0.25 to 1
- gate_weight: bfloat16 [3584, 4096], P(None, 'expert'), may hold values from -0.09375 to 0.09375
- up_weight: bfloat16 [3584, 4096], P(None, 'expert'), may hold values from -0.09375 to 0.09375
- down_weight: bfloat16 [4096, 3584], P('expert'), may hold values from -0.1875 to 0.1875
Outputs:
- combined: bfloat16 [4096, 3584], P(('groups', 'expert')), parts along dimension 0
There are 2 independent parts, one for each index of `groups`. A program takes and returns all parts, laid end to end along the dimension named above; an argument that names none is the same for every part. Nothing has to cross between parts.
Inputs may be any that keep to these rules, and one draw needn't show every extreme that they name: `routes`: each row names 2 different experts; in the rows of one device no expert is named more than 96 times, and in some block some expert exactly 96 times.
All inputs are finite; a program needn't handle non-finite values.
Results may differ from a plain program's by a relative error of at most 0.0071.
Values may be sent and summed in bfloat16 or wider, within the bound.
A program may use at most 128 MiB of HBM per device.

v0:
```python
import jax
import jax.numpy as jnp
from jax import lax
from jax.sharding import PartitionSpec as P

HB = 128
SHARDS = 4


def hadamard(size):
    counter = jnp.arange(size, dtype=jnp.int32)
    parity = jnp.zeros((size, size), jnp.int32)
    for bit_level in range(size.bit_length() - 1):
        parity = parity + (counter[:, None] >> bit_level & counter[None, :] >> bit_level & 1)
    return (1 - 2 * (parity % 2)).astype(jnp.bfloat16)


def rotate(tokens):
    row_count, width = tokens.shape
    blocked = tokens.reshape(row_count, width // HB, HB)
    turned = jnp.einsum("tbi,ij->tbj", blocked, hadamard(HB), preferred_element_type=jnp.float32)
    return (turned * (1.0 / HB**0.5)).astype(jnp.bfloat16).reshape(row_count, width)


def on_device(tokens, routes, gates, gate_weight, up_weight, down_weight):
    devices = lax.axis_size("expert")
    resident = devices // SHARDS
    row_count, width = tokens.shape
    per_token = routes.shape[1]
    capacity = SHARDS * max(1, 3 * row_count * per_token // (2 * resident * SHARDS))
    rotated = rotate(tokens)
    flat_routes = routes.reshape(-1)
    onehot = (flat_routes[:, None] == jnp.arange(resident, dtype=jnp.int32)[None, :]).astype(
        jnp.int32
    )
    running = jnp.cumsum(onehot, axis=0) - onehot
    slot = jnp.sum(running * onehot, axis=1)
    target_slot = flat_routes * capacity + slot
    owners = jnp.arange(row_count * per_token, dtype=jnp.int32) // per_token
    owner_table = jnp.full((resident * capacity,), row_count, jnp.int32).at[target_slot].set(owners)
    padded = jnp.concatenate([rotated, jnp.zeros((1, width), jnp.bfloat16)], 0)
    buckets = padded[owner_table].reshape(resident, capacity, width)
    copies = jnp.broadcast_to(buckets[:, None], (resident, SHARDS, capacity, width)).reshape(
        devices, capacity, width
    )
    received = lax.all_to_all(copies, "expert", split_axis=0, concat_axis=0, tiled=True)
    slot_rows = received.reshape(-1, width)
    gate_act = jnp.dot(slot_rows, gate_weight, preferred_element_type=jnp.float32)
    up_act = jnp.dot(slot_rows, up_weight, preferred_element_type=jnp.float32)
    hidden = (jax.nn.silu(gate_act) * up_act).astype(jnp.bfloat16)
    partial_value = jnp.dot(hidden, down_weight, preferred_element_type=jnp.float32).astype(
        jnp.bfloat16
    )
    partial_value = partial_value.reshape(received.shape)
    returned = lax.all_to_all(partial_value, "expert", split_axis=0, concat_axis=0, tiled=True)
    expert_out = jnp.sum(
        returned.reshape(resident, SHARDS, capacity, width).astype(jnp.float32), axis=1
    )
    expert_out = expert_out.reshape(resident * capacity, width)
    picked = expert_out[target_slot].reshape(row_count, per_token, width)
    return jnp.sum(gates[:, :, None] * picked, axis=1).astype(jnp.bfloat16)


def solution(mesh):
    in_specs = (
        P(("groups", "expert"), None),
        P(("groups", "expert"), None),
        P(("groups", "expert"), None),
        P(None, "expert"),
        P(None, "expert"),
        P("expert", None),
    )
    out_specs = P(("groups", "expert"), None)
    return jax.shard_map(
        on_device, mesh=mesh, in_specs=in_specs, out_specs=out_specs, check_vma=False
    )
```

profile of v0, /device:TPU:11, one launch (start us, length us, event | category | flops | bytes accessed | tf_op | source)
XLA Modules:
  0.0 568.4 jit_solution(707087954741286223)
XLA Ops:
  0.0 0.9 copy.17
  0.9 0.1 eq.31
  1.1 0.1 eq.27
  1.2 0.7 broadcast_multiply_fusion
  1.9 1.5 copy.13
  3.5 1.5 multiply_convert_fusion
  5.0 2.2 copy.15
  7.2 1.2 reduce-window.6
  8.9 0.1 mul.51
  9.1 1.4 scatter_custom_fusion
  10.5 1.2 concatenate.3
  11.8 3.9 gather_fusion
  15.7 7.0 %broadcast_in_dim.11 = bf16[4,4,96,3584]{3,2,1,0:T(8,128)(2,1)} broadcast(bf16[4,96,3584]{2,1,0:T(8,128)(2,1)} %bitcast.44), dimensions={0,2,3} | broadcast | bytes 13762560 | tf_op jit(solution)/shard_map/broadcast_in_dim | solution.py:43
  22.7 245.0 %all_to_all.10 = bf16[16,96,3584]{2,1,0:T(8,128)(2,1)S(1)} all-to-all(bf16[16,96,3584]{2,1,0:T(8,128)(2,1)} %bitcast.43), channel_id=1, replica_groups=mesh['groups'=2,'expert'=16] {'expert'}, dimensions={0} | all-to-all | bytes 22020096 | tf_op jit(solution)/shard_map/all_to_all | solution.py:46
  267.7 4.0 copy-done.2
  271.7 4.2 fusion.39
  276.0 17.4 %convolution_convert_fusion = bf16[1536,3584]{1,0:T(8,128)(2,1)} fusion(bf16[256,3584]{1,0:T(8,128)(2,1)S(1)} %copy-done, bf16[1536,3584]{1,0:T(8,128)(2,1)} %bitcast.47, bf16[3584,256]{1,0:T(8,128)(2,1)} %param.10, f32[1536,256]{1,0:T(8,128)} %fusion.39), kind=kOutput, calls=%fused_computation.4 | convolution fusion | flops 5645008896 | bytes 27262976 | tf_op jit(solution)/shard_map/dot_general | solution.py:51
  293.4 6.1 %all-to-all-start.1 = ((bf16[16,96,3584]{2,1,0:T(8,128)(2,1)}), bf16[16,96,3584]{2,1,0:T(8,128)(2,1)}, u32[]{:S(2)}, u32[]{:S(2)}) async-start(bf16[16,96,3584]{2,1,0:T(8,128)(2,1)} %bitcast.45), calls=%async_computation.1 | async-start | bytes 22020096 | tf_op jit(solution)/shard_map/all_to_all | solution.py:55
  299.5 0.1 copy.12
  299.6 238.4 %all-to-all-done.1 = bf16[16,96,3584]{2,1,0:T(8,128)(2,1)} async-done(((bf16[16,96,3584]{2,1,0:T(8,128)(2,1)}), bf16[16,96,3584]{2,1,0:T(8,128)(2,1)}, u32[]{:S(2)}, u32[]{:S(2)}) %all-to-all-start.1) | async-done | bytes 11010080 | tf_op jit(solution)/shard_map/all_to_all | solution.py:55
  538.0 8.8 %convert_reduce_fusion = f32[4,96,3584]{2,1,0:T(8,128)} fusion(bf16[16,96,3584]{2,1,0:T(8,128)(2,1)} %all-to-all-done.1), kind=kLoop, calls=%fused_computation.3 | loop fusion | flops 9633792 | bytes 16515072 | tf_op jit(solution)/shard_map/reduce_sum | solution.py:56
  546.8 7.8 %gather_fusion.1 = f32[256,3584]{1,0:T(8,128)} fusion(f32[384,3584]{1,0:T(8,128)} %bitcast.42, s32[1024]{0:T(1024)S(1)} %pad_clamp_fusion), kind=kCustom, calls=%fused_computation.1 | custom fusion | bytes 7341056 | tf_op jit(solution)/shard_map/gather | solution.py:60
  554.6 5.6 reshape.149
  560.2 8.2 %multiply_reduce_fusion = bf16[128,3584]{1,0:T(8,128)(2,1)} fusion(f32[128,2,3584]{2,1,0:T(2,128)} %reshape.149, f32[128,2]{1,0:T(8,128)S(1)} %copy.12), kind=kLoop, calls=%fused_computation.5 | loop fusion | flops 1376256 | bytes 4588544 | tf_op jit(solution)/shard_map/reduce_sum | solution.py:61
  (27 shorter events, 0.6 us)
Async XLA Ops:
  0.0 276.0 %copy-start = (bf16[256,3584]{1,0:T(8,128)(2,1)S(1)}, bf16[256,3584]{1,0:T(8,128)(2,1)}, u32[]{:S(2)}) copy-start(bf16[256,3584]{1,0:T(8,128)(2,1)} %param.11) | copy-start | bytes 5505028
  22.7 249.0 %copy-start.4 = (bf16[3584,256]{1,0:T(8,128)(2,1)S(1)}, bf16[3584,256]{1,0:T(8,128)(2,1)}, u32[]{:S(2)}) copy-start(bf16[3584,256]{1,0:T(8,128)(2,1)} %param.9) | copy-start | bytes 5505028
  267.7 4.0 copy-start.2
  293.3 6.1 %copy-start.3 = (f32[128,2]{0,1:T(2,128)S(1)}, f32[128,2]{0,1:T(2,128)}, u32[]{:S(2)}) copy-start(f32[128,2]{0,1:T(2,128)} %param.8) | copy-start | bytes 3076
  293.4 244.6 %all-to-all-start.1 = ((bf16[16,96,3584]{2,1,0:T(8,128)(2,1)}), bf16[16,96,3584]{2,1,0:T(8,128)(2,1)}, u32[]{:S(2)}, u32[]{:S(2)}) async-start(bf16[16,96,3584]{2,1,0:T(8,128)(2,1)} %bitcast.45), calls=%async_computation.1 | async-start | bytes 22020096 | tf_op jit(solution)/shard_map/all_to_all | solution.py:55
  554.6 13.9 %copy-start.1 = (bf16[256,3584]{1,0:T(8,128)(2,1)S(1)}, bf16[256,3584]{1,0:T(8,128)(2,1)}, u32[]{:S(2)}) copy-start(bf16[256,3584]{1,0:T(8,128)(2,1)} %param.11) | copy-start | bytes 5505028
where the time goes:
time: 569 us; the launch traced here: 568 us
  blocking collectives  245 us (43%)
  waiting for transfers between devices  238 us (42%)
  local copies, waits for them, and re-layouts  36.7 us (6%)
  matrix products  23.1 us (4%)
  other arithmetic  19.1 us (3%)
  starting transfers between devices  6.1 us (1%)
    all_to_all x1, blocking collectives, on_device(): lax.all_to_all(copies, 'expert', split_axis=0, concat_axis=0, tiled=True)  245 us
    all_to_all x1, waiting for transfers between devices, on_device(): lax.all_to_all(partial_value, 'expert', split_axis=0, concat_axis=0, tile...  238 us
    dot_general x1, matrix products, on_device(): jnp.dot(hidden, down_weight, preferred_element_type=jnp.float32)  17.4 us
  transfers between devices with their start and end apart: 1, of which 1 were waited for; matrix products, arithmetic and copies ran while one was open for 0% of the time, Pallas kernels for 0%

commit v1 on v0

--- a/solution.py
+++ b/solution.py
@@ -1,10 +1,15 @@
+import functools
 import jax
 import jax.numpy as jnp
 from jax import lax
+from jax.experimental import pallas as pl
+from jax.experimental.pallas import tpu as pltpu
 from jax.sharding import PartitionSpec as P
 
 HB = 128
 SHARDS = 4
+AHEAD = 2
+MESH = pl.DeviceIdType.MESH
 
 
 def hadamard(size):
@@ -13,6 +18,384 @@
     for bit_level in range(size.bit_length() - 1):
         parity = parity + (counter[:, None] >> bit_level & counter[None, :] >> bit_level & 1)
     return (1 - 2 * (parity % 2)).astype(jnp.bfloat16)
+
+
+def layer_kernel(
+    planes, steps, tok_ref, wt_ref, had_ref, gate_ref, up_ref, down_ref, out_ref,
+    tok, wts, wcol, gu, dn, hid, acc, from_lo, from_hi, outbox,
+    own_sem, x_s, x_r, y_s, y_r, co_s, co_r, cx_s, cx_r, cy_s, cy_r,
+    tu_s, td_s, t_r, wu_s, wd_s, w_r, r_s, lo_r, hi_r,
+):
+    me = lax.axis_index("expert")
+    y = lax.axis_index("groups")
+    z, x, c = me // 4, (me // 2) % 2, me % 2
+    top = planes - 1
+    rows, width = tok_ref.shape
+    units = gate_ref.shape[1]
+    shard, xshard = 2 * x + c, 2 * (1 - x) + c
+    xpeer, cpeer = {"expert": z * 4 + xshard}, {"expert": z * 4 + 2 * x + 1 - c}
+    ypeer = {"groups": 1 - y}
+    hi_peer, lo_peer = {"expert": me + 4}, {"expert": me - 4}
+    wrows, wcols = width // 2 // steps, width // steps
+    cols = lambda q: pl.ds(pl.multiple_of(q * wcols, wcols), wcols)
+
+    barrier = pltpu.get_barrier_semaphore()
+    for peer in (xpeer, cpeer, ypeer):
+        pl.semaphore_signal(barrier, inc=1, device_id=peer, device_id_type=MESH)
+
+    @pl.when(z > 0)
+    def _():
+        pl.semaphore_signal(barrier, inc=1, device_id=lo_peer, device_id_type=MESH)
+
+    @pl.when(z < top)
+    def _():
+        pl.semaphore_signal(barrier, inc=1, device_id=hi_peer, device_id_type=MESH)
+
+    pl.semaphore_wait(barrier, 3 + jnp.where(z > 0, 1, 0) + jnp.where(z < top, 1, 0))
+
+    def remote(src, dst, send, recv, peer):
+        return pltpu.make_async_remote_copy(
+            src_ref=src, dst_ref=dst, send_sem=send, recv_sem=recv,
+            device_id=peer, device_id_type=MESH)
+
+    def piece(kind, part, half, k):
+        if kind < 2:
+            row = pl.multiple_of(half * (width // 2) + k * wrows, wrows)
+            return gu.at[part, kind, pl.ds(row, wrows), :]
+        row = pl.multiple_of(part * units + half * (units // 2), units // 2)
+        return dn.at[pl.ds(row, units // 2), cols(k)]
+
+    def own_piece(kind, half, k):
+        if kind < 2:
+            row = pl.multiple_of(half * (width // 2) + k * wrows, wrows)
+            return (gate_ref, up_ref)[kind].at[pl.ds(row, wrows), :]
+        row = pl.multiple_of(half * (units // 2), units // 2)
+        return down_ref.at[pl.ds(row, units // 2), cols(k)]
+
+    def x_copy(kind, k):
+        return remote(own_piece(kind, y, k), piece(kind, shard, y, k),
+                      x_s.at[kind, k], x_r.at[kind, k], xpeer)
+
+    def y_copy(kind, k):
+        got = piece(kind, xshard, y, k)
+        return remote(got, got, y_s.at[kind, k], y_r.at[kind, k], ypeer)
+
+    def cx_copy(kind, k):
+        got = piece(kind, xshard, y, k)
+        return remote(got, got, cx_s.at[kind, k], cx_r.at[kind, k], cpeer)
+
+    def cy_copy(kind, k):
+        got = piece(kind, xshard, 1 - y, k)
+        return remote(got, got, cy_s.at[kind, k], cy_r.at[kind, k], cpeer)
+
+    own_rows = pl.ds(pl.multiple_of(shard * units, units), units)
+
+    def own_to(kind):
+        return (gu.at[shard, 0], gu.at[shard, 1], dn.at[own_rows, :])[kind]
+
+    weights = (gate_ref, up_ref, down_ref)
+
+    def own_core(kind):
+        return remote(weights[kind], own_to(kind), co_s.at[kind], co_r.at[kind], cpeer)
+
+    def own_local(kind):
+        return pltpu.make_async_copy(weights[kind], own_to(kind), own_sem.at[kind])
+
+    def tok_copy(block, q, up):
+        part = tok.at[block, :, cols(q)]
+        return remote(part, part, (tu_s if up else td_s).at[block, q], t_r.at[block, q],
+                      hi_peer if up else lo_peer)
+
+    def w_copy(block, up):
+        part = wts.at[block]
+        return remote(part, part, (wu_s if up else wd_s).at[block], w_r.at[block],
+                      hi_peer if up else lo_peer)
+
+    def ret_copy(home, q, up):
+        return remote(outbox.at[home, :, cols(q)], (from_lo if up else from_hi).at[home, :, cols(q)],
+                      r_s.at[home, q], (lo_r if up else hi_r).at[home, q],
+                      hi_peer if up else lo_peer)
+
+    for k in range(AHEAD):
+        for kind in (0, 1):
+            x_copy(kind, k).start()
+    wts[z] = wt_ref[...]
+
+    @pl.when(z < top)
+    def _():
+        w_copy(z, True).start()
+
+    @pl.when(z > 0)
+    def _():
+        w_copy(z, False).start()
+
+    had = had_ref[...]
+
+    @pl.loop(0, steps)
+    def _(q):
+        for b in range(wcols // HB):
+            at = pl.ds(pl.multiple_of(q * wcols + b * HB, HB), HB)
+            turned = jnp.dot(tok_ref[:, at], had, preferred_element_type=jnp.float32)
+            tok[z, :, at] = (turned * (1.0 / HB**0.5)).astype(jnp.bfloat16)
+
+        @pl.when(z < top)
+        def _():
+            tok_copy(z, q, True).start()
+
+        @pl.when(z > 0)
+        def _():
+            tok_copy(z, q, False).start()
+
+    for kind in range(3):
+        own_local(kind).start()
+        own_core(kind).start()
+
+    def relay(r, q):
+        lo, hi = z - r, z + r
+
+        @pl.when(lo >= 0)
+        def _():
+            tok_copy(lo, q, True).wait_recv()
+
+            @pl.when(q == 0)
+            def _():
+                w_copy(lo, True).wait_recv()
+
+            @pl.when(z < top)
+            def _():
+                tok_copy(lo, q, True).start()
+
+                @pl.when(q == 0)
+                def _():
+                    w_copy(lo, True).start()
+
+        @pl.when(hi <= top)
+        def _():
+            tok_copy(hi, q, False).wait_recv()
+
+            @pl.when(q == 0)
+            def _():
+                w_copy(hi, False).wait_recv()
+
+            @pl.when(z > 0)
+            def _():
+                tok_copy(hi, q, False).start()
+
+                @pl.when(q == 0)
+                def _():
+                    w_copy(hi, False).start()
+
+    def pass_x(kind, k):
+        x_copy(kind, k).wait_recv()
+        y_copy(kind, k).start()
+        cx_copy(kind, k).start()
+
+    def pass_y(kind, k):
+        y_copy(kind, k).wait_recv()
+        cy_copy(kind, k).start()
+
+    @pl.loop(0, steps)
+    def _(k):
+        for kind in (0, 1):
+            pass_x(kind, k)
+
+            @pl.when(k < steps - AHEAD)
+            def _():
+                x_copy(kind, k + AHEAD).start()
+
+            @pl.when(k >= steps - AHEAD)
+            def _():
+                if kind == 0:
+                    x_copy(2, 2 * (k - (steps - AHEAD))).start()
+                else:
+                    x_copy(2, 2 * (k - (steps - AHEAD)) + 1).start()
+
+            @pl.when(k > 0)
+            def _():
+                pass_y(kind, k - 1)
+
+            t = 2 * k + kind
+            relay(t // steps + 1, t % steps)
+
+    for kind in (0, 1):
+        pass_y(kind, steps - 1)
+
+    def wait_weights(kind):
+        own_local(kind).wait()
+        own_core(kind).wait_recv()
+
+        @pl.loop(0, steps)
+        def _(k):
+            cx_copy(kind, k).wait_recv()
+            cy_copy(kind, k).wait_recv()
+
+    turn = jnp.where(z < planes // 2, 1, planes - 1)
+    home_of = lambda p: lax.rem(z + turn * p, planes)
+
+    def make_hidden(p):
+        block = home_of(p)
+        lane = lax.broadcasted_iota(jnp.int32, (8, rows), 0)
+        row = jnp.sum(jnp.where(lane == z, wts[block], 0.0), axis=0, keepdims=True)
+        wcol[p] = jnp.transpose(jnp.broadcast_to(row, (rows, rows)))
+
+        @pl.loop(0, SHARDS)
+        def _(s):
+            g = jnp.dot(tok[block], gu[s, 0], preferred_element_type=jnp.float32)
+            u = jnp.dot(tok[block], gu[s, 1], preferred_element_type=jnp.float32)
+            h = (g / (1.0 + jnp.exp(-g))) * u
+            hid[p, :, pl.ds(pl.multiple_of(s * units, units), units)] = h.astype(jnp.bfloat16)
+
+    wait_weights(0)
+    wait_weights(1)
+
+    @pl.loop(0, steps)
+    def _(k):
+        pass_x(2, k)
+
+        @pl.when(k + 2 * AHEAD < steps)
+        def _():
+            x_copy(2, k + 2 * AHEAD).start()
+
+        @pl.when(k > 0)
+        def _():
+            pass_y(2, k - 1)
+
+        relay(planes - 1, k)
+
+        @pl.when(k % 2 == 0)
+        def _():
+            @pl.when(k < 2 * (planes - 1))
+            def _():
+                make_hidden(k // 2)
+
+    pass_y(2, steps - 1)
+    wait_weights(2)
+
+    def expert_rows(p, q):
+        val = jnp.dot(hid[p], dn[:, cols(q)], preferred_element_type=jnp.float32)
+        w = wcol[p]
+        for b in range(wcols // HB):
+            acc[:, b * HB:(b + 1) * HB] = val[:, b * HB:(b + 1) * HB] * w
+
+    def give_back(p):
+        home = home_of(p)
+
+        @pl.loop(0, steps)
+        def _(q):
+            expert_rows(p, q)
+
+            @pl.when((home > z) & (z > 0))
+            def _():
+                ret_copy(home, q, True).wait_recv()
+                acc[...] += from_lo[home, :, cols(q)].astype(jnp.float32)
+
+            @pl.when((home < z) & (z < top))
+            def _():
+                ret_copy(home, q, False).wait_recv()
+                acc[...] += from_hi[home, :, cols(q)].astype(jnp.float32)
+
+            outbox[home, :, cols(q)] = acc[...].astype(jnp.bfloat16)
+
+            @pl.when(home > z)
+            def _():
+                ret_copy(home, q, True).start()
+
+            @pl.when(home < z)
+            def _():
+                ret_copy(home, q, False).start()
+
+    @pl.loop(1, planes)
+    def _(p):
+        @pl.when(p == planes - 1)
+        def _():
+            make_hidden(p)
+
+        give_back(p)
+
+    @pl.loop(0, steps)
+    def _(q):
+        expert_rows(0, q)
+
+        @pl.when(z > 0)
+        def _():
+            ret_copy(z, q, True).wait_recv()
+            acc[...] += from_lo[z, :, cols(q)].astype(jnp.float32)
+
+        @pl.when(z < top)
+        def _():
+            ret_copy(z, q, False).wait_recv()
+            acc[...] += from_hi[z, :, cols(q)].astype(jnp.float32)
+
+        out_ref[:, cols(q)] = acc[...].astype(jnp.bfloat16)
+
+    for kind in range(3):
+        own_core(kind).wait_send()
+
+        @pl.loop(0, steps)
+        def _(k):
+            x_copy(kind, k).wait_send()
+            y_copy(kind, k).wait_send()
+            cx_copy(kind, k).wait_send()
+            cy_copy(kind, k).wait_send()
+
+    @pl.loop(0, planes)
+    def _(block):
+        for up in (True, False):
+            @pl.when((z < top) & (block <= z) if up else (z > 0) & (block >= z))
+            def _():
+                w_copy(block, up).wait_send()
+
+                @pl.loop(0, steps)
+                def _(q):
+                    tok_copy(block, q, up).wait_send()
+
+        @pl.when(block != z)
+        def _():
+            @pl.loop(0, steps)
+            def _(q):
+                ret_copy(block, q, True).wait_send()
+
+
+def on_slice(planes, tokens, routes, gates, gate_weight, up_weight, down_weight):
+    rows, width = tokens.shape
+    units = gate_weight.shape[1]
+    steps = 7
+    lanes = jnp.arange(8, dtype=jnp.int32)[:, None, None]
+    wt = jnp.sum(jnp.where(routes[None] == lanes, gates[None], 0.0), axis=2)
+    vmem = pl.BlockSpec(memory_space=pltpu.VMEM)
+    anywhere = pl.BlockSpec(memory_space=pl.ANY)
+    dma = pltpu.SemaphoreType.DMA
+    bf16, f32 = jnp.bfloat16, jnp.float32
+    return pl.pallas_call(
+        functools.partial(layer_kernel, planes, steps),
+        out_shape=jax.ShapeDtypeStruct((rows, width), bf16),
+        in_specs=[vmem] * 3 + [anywhere] * 3,
+        out_specs=vmem,
+        scratch_shapes=[
+            pltpu.VMEM((planes, rows, width), bf16),
+            pltpu.VMEM((planes, 8, rows), f32),
+            pltpu.VMEM((planes, rows, rows), f32),
+            pltpu.VMEM((SHARDS, 2, width, units), bf16),
+            pltpu.VMEM((SHARDS * units, width), bf16),
+            pltpu.VMEM((planes, rows, SHARDS * units), bf16),
+            pltpu.VMEM((rows, width // steps), f32),
+            pltpu.VMEM((planes, rows, width), bf16),
+            pltpu.VMEM((planes, rows, width), bf16),
+            pltpu.VMEM((planes, rows, width), bf16),
+            dma((3,)),
+            dma((3, steps)), dma((3, steps)),
+            dma((3, steps)), dma((3, steps)),
+            dma((3,)), dma((3,)),
+            dma((3, steps)), dma((3, steps)),
+            dma((3, steps)), dma((3, steps)),
+            dma((planes, steps)), dma((planes, steps)), dma((planes, steps)),
+            dma((planes,)), dma((planes,)), dma((planes,)),
+            dma((planes, steps)), dma((planes, steps)), dma((planes, steps)),
+        ],
+        compiler_params=pltpu.CompilerParams(
+            collective_id=0, has_side_effects=True, vmem_limit_bytes=56 * 2**20
+        ),
+    )(tokens, wt, hadamard(HB), gate_weight, up_weight, down_weight)
 
 
 def rotate(tokens):
@@ -62,6 +445,11 @@
 
 
 def solution(mesh):
+    devices = mesh.shape["expert"]
+    planes = devices // SHARDS
+    body = on_device
+    if devices == 16 and mesh.shape["groups"] == 2:
+        body = functools.partial(on_slice, planes)
     in_specs = (
         P(("groups", "expert"), None),
         P(("groups", "expert"), None),
@@ -72,5 +460,5 @@
     )
     out_specs = P(("groups", "expert"), None)
     return jax.shard_map(
-        on_device, mesh=mesh, in_specs=in_specs, out_specs=out_specs, check_vma=False
-    )
+        body, mesh=mesh, in_specs=in_specs, out_specs=out_specs, check_vma=False
+    )

time: 569 us -> 174 us (0.31)
  the two profiles are of different devices: /device:TPU:11 before, /device:TPU:0 now
where the time goes in v1:
time: 174 us
  Pallas kernels  169 us (97%)
  local copies, waits for them, and re-layouts  2.16 us (1%)
  other arithmetic  2.11 us (1%)
    pallas_call x1, Pallas kernels, on_slice(): pl.pallas_call(functools.partial(layer_kernel, planes, steps), out_shape=...  169 us

profile of v1, /device:TPU:0, one launch (start us, length us, event | category | flops | bytes accessed | tf_op | source)
XLA Modules:
  0.0 173.6 jit_solution(5509601084753261181)
XLA Ops:
  0.0 1.3 select_reduce_fusion.wt_ref
  1.3 0.8 fusion.3.had_ref
  2.1 169.3 %shard_map.64 = bf16[128,3584]{1,0:T(8,128)(2,1)} custom-call(bf16[128,3584]{1,0:T(8,128)(2,1)} %tok_ref.1, f32[8,128]{1,0:T(8,128)} %select_reduce_fusion.wt_ref, bf16[128,128]{1,0:T(8,128)(2,1)} %fusion.3.had_ref, bf16[3584,256]{1,0:T(8,128)(2,1)} %gate_ref.1, bf16[3584,256]{1,0:T(8,128)(2,1)} %up_ref.1, bf16[256,3584]{1,0:T(8,128)(2,1)} %down_ref.1), custom_call_target="tpu_custom_call" | custom-call | tf_op jit(solution)/shard_map/pallas_call | solution.py:369
  171.4 2.2 %copy.10 = bf16[128,3584]{1,0:T(8,128)(2,1)} copy(bf16[128,3584]{1,0:T(8,128)(2,1)} %shard_map.64) | data formatting | bytes 1835008
  (4 shorter events, 0.0 us)

commit v2 on v1

--- a/solution.py
+++ b/solution.py
@@ -8,7 +8,7 @@
 
 HB = 128
 SHARDS = 4
-AHEAD = 2
+AHEAD = 3
 MESH = pl.DeviceIdType.MESH
 
 
@@ -229,8 +229,12 @@
             cx_copy(kind, k).wait_recv()
             cy_copy(kind, k).wait_recv()
 
-    turn = jnp.where(z < planes // 2, 1, planes - 1)
-    home_of = lambda p: lax.rem(z + turn * p, planes)
+    low = z < planes // 2
+
+    def home_of(p):
+        across = jnp.where(p == 1, jnp.where(low, 2, 1), jnp.where(low, 3, 0))
+        beside = jnp.where(low, 1 - z, 5 - z)
+        return jnp.where(p == 0, z, jnp.where(p == 3, beside, across))
 
     def make_hidden(p):
         block = home_of(p)
@@ -245,72 +249,78 @@
             h = (g / (1.0 + jnp.exp(-g))) * u
             hid[p, :, pl.ds(pl.multiple_of(s * units, units), units)] = h.astype(jnp.bfloat16)
 
-    wait_weights(0)
-    wait_weights(1)
-
-    @pl.loop(0, steps)
-    def _(k):
-        pass_x(2, k)
-
-        @pl.when(k + 2 * AHEAD < steps)
-        def _():
-            x_copy(2, k + 2 * AHEAD).start()
-
-        @pl.when(k > 0)
-        def _():
-            pass_y(2, k - 1)
-
-        relay(planes - 1, k)
-
-        @pl.when(k % 2 == 0)
-        def _():
-            @pl.when(k < 2 * (planes - 1))
-            def _():
-                make_hidden(k // 2)
-
-    pass_y(2, steps - 1)
-    wait_weights(2)
-
     def expert_rows(p, q):
         val = jnp.dot(hid[p], dn[:, cols(q)], preferred_element_type=jnp.float32)
         w = wcol[p]
         for b in range(wcols // HB):
             acc[:, b * HB:(b + 1) * HB] = val[:, b * HB:(b + 1) * HB] * w
 
-    def give_back(p):
+    def give_back(p, q):
         home = home_of(p)
+        expert_rows(p, q)
+
+        @pl.when((home > z) & (z > 0))
+        def _():
+            ret_copy(home, q, True).wait_recv()
+            acc[...] += from_lo[home, :, cols(q)].astype(jnp.float32)
+
+        @pl.when((home < z) & (z < top))
+        def _():
+            ret_copy(home, q, False).wait_recv()
+            acc[...] += from_hi[home, :, cols(q)].astype(jnp.float32)
+
+        outbox[home, :, cols(q)] = acc[...].astype(jnp.bfloat16)
+
+        @pl.when(home > z)
+        def _():
+            ret_copy(home, q, True).start()
+
+        @pl.when(home < z)
+        def _():
+            ret_copy(home, q, False).start()
+
+    wait_weights(0)
+    wait_weights(1)
+    own_local(2).wait()
+    own_core(2).wait_recv()
+    make_hidden(1)
+
+    def first_back(q):
+        cx_copy(2, q).wait_recv()
+        cy_copy(2, q).wait_recv()
+        give_back(1, q)
+
+    @pl.loop(0, steps)
+    def _(k):
+        pass_x(2, k)
+
+        @pl.when(k + 2 * AHEAD < steps)
+        def _():
+            x_copy(2, k + 2 * AHEAD).start()
+
+        @pl.when(k > 0)
+        def _():
+            pass_y(2, k - 1)
+
+        relay(planes - 1, k)
+
+        @pl.when(k > 1)
+        def _():
+            first_back(k - 2)
+
+    pass_y(2, steps - 1)
+    first_back(steps - 2)
+    first_back(steps - 1)
+
+    @pl.loop(2, planes)
+    def _(p):
+        make_hidden(p)
 
         @pl.loop(0, steps)
         def _(q):
-            expert_rows(p, q)
-
-            @pl.when((home > z) & (z > 0))
-            def _():
-                ret_copy(home, q, True).wait_recv()
-                acc[...] += from_lo[home, :, cols(q)].astype(jnp.float32)
-
-            @pl.when((home < z) & (z < top))
-            def _():
-                ret_copy(home, q, False).wait_recv()
-                acc[...] += from_hi[home, :, cols(q)].astype(jnp.float32)
-
-            outbox[home, :, cols(q)] = acc[...].astype(jnp.bfloat16)
-
-            @pl.when(home > z)
-            def _():
-                ret_copy(home, q, True).start()
-
-            @pl.when(home < z)
-            def _():
-                ret_copy(home, q, False).start()
-
-    @pl.loop(1, planes)
-    def _(p):
-        @pl.when(p == planes - 1)
-        def _():
-            make_hidden(p)
-
-        give_back(p)
+            give_back(p, q)
+
+    make_hidden(0)
 
     @pl.loop(0, steps)
     def _(q):

time: 174 us -> 137 us (0.79)
  Pallas kernels: 169 us -> 133 us
    pallas_call x1, Pallas kernels: 169 us -> 133 us  [on_slice(): pl.pallas_call(functools.partial(layer_kernel, planes, steps), out_shape=...]
where the time goes in v2:
time: 137 us
  Pallas kernels  133 us (97%)
  local copies, waits for them, and re-layouts  2.16 us (2%)
  other arithmetic  2.11 us (2%)
    pallas_call x1, Pallas kernels, on_slice(): pl.pallas_call(functools.partial(layer_kernel, planes, steps), out_shape=...  133 us

profile of v2, /device:TPU:0, one launch (start us, length us, event | category | flops | bytes accessed | tf_op | source)
XLA Modules:
  0.0 137.1 jit_solution(5569371708391799354)
XLA Ops:
  0.0 1.3 select_reduce_fusion.wt_ref
  1.3 0.8 fusion.3.had_ref
  2.1 132.8 %shard_map.64 = bf16[128,3584]{1,0:T(8,128)(2,1)} custom-call(bf16[128,3584]{1,0:T(8,128)(2,1)} %tok_ref.1, f32[8,128]{1,0:T(8,128)} %select_reduce_fusion.wt_ref, bf16[128,128]{1,0:T(8,128)(2,1)} %fusion.3.had_ref, bf16[3584,256]{1,0:T(8,128)(2,1)} %gate_ref.1, bf16[3584,256]{1,0:T(8,128)(2,1)} %up_ref.1, bf16[256,3584]{1,0:T(8,128)(2,1)} %down_ref.1), custom_call_target="tpu_custom_call" | custom-call | tf_op jit(solution)/shard_map/pallas_call | solution.py:379
  134.9 2.2 %copy.10 = bf16[128,3584]{1,0:T(8,128)(2,1)} copy(bf16[128,3584]{1,0:T(8,128)(2,1)} %shard_map.64) | data formatting | bytes 1835008
  (4 shorter events, 0.0 us)

commit v3 on v2

--- a/solution.py
+++ b/solution.py
@@ -21,8 +21,8 @@
 
 
 def layer_kernel(
-    planes, steps, tok_ref, wt_ref, had_ref, gate_ref, up_ref, down_ref, out_ref,
-    tok, wts, wcol, gu, dn, hid, acc, from_lo, from_hi, outbox,
+    planes, steps, cap, tok_ref, wt_ref, had_ref, gate_ref, up_ref, down_ref, out_ref,
+    tok, wts, wcol, place, gu, dn, hid, acc, from_lo, from_hi, outbox,
     own_sem, x_s, x_r, y_s, y_r, co_s, co_r, cx_s, cx_r, cy_s, cy_r,
     tu_s, td_s, t_r, wu_s, wd_s, w_r, r_s, lo_r, hi_r,
 ):
@@ -111,8 +111,10 @@
         return remote(part, part, (wu_s if up else wd_s).at[block], w_r.at[block],
                       hi_peer if up else lo_peer)
 
-    def ret_copy(home, q, up):
-        return remote(outbox.at[home, :, cols(q)], (from_lo if up else from_hi).at[home, :, cols(q)],
+    def ret_copy(home, q, up, n):
+        some = pl.ds(0, n)
+        return remote(outbox.at[home, some, cols(q)],
+                      (from_lo if up else from_hi).at[home, some, cols(q)],
                       r_s.at[home, q], (lo_r if up else hi_r).at[home, q],
                       hi_peer if up else lo_peer)
 
@@ -236,12 +238,23 @@
         beside = jnp.where(low, 1 - z, 5 - z)
         return jnp.where(p == 0, z, jnp.where(p == 3, beside, across))
 
+    end = (z == 0) | (z == top)
+    packs = lambda p: end & (p != 0)
+
+    def expert_row(block, expert):
+        at = lax.broadcasted_iota(jnp.int32, (8, rows), 0)
+        return jnp.sum(jnp.where(at == expert, wts[block], 0.0), axis=0, keepdims=True)
+
+    def slots(weight):
+        down, across = (lax.broadcasted_iota(jnp.int32, (rows, rows), d) for d in (0, 1))
+        chosen = jnp.where(weight > 0.0, 1.0, 0.0)
+        before = jnp.where(down < across, 1.0, 0.0).astype(jnp.bfloat16)
+        slot = jnp.dot(jnp.broadcast_to(chosen, (16, rows)).astype(jnp.bfloat16), before,
+                       preferred_element_type=jnp.float32)[:1]
+        return jnp.where(down.astype(jnp.float32) == slot, chosen, 0.0)
+
     def make_hidden(p):
         block = home_of(p)
-        lane = lax.broadcasted_iota(jnp.int32, (8, rows), 0)
-        row = jnp.sum(jnp.where(lane == z, wts[block], 0.0), axis=0, keepdims=True)
-        wcol[p] = jnp.transpose(jnp.broadcast_to(row, (rows, rows)))
-
         @pl.loop(0, SHARDS)
         def _(s):
             g = jnp.dot(tok[block], gu[s, 0], preferred_element_type=jnp.float32)
@@ -249,35 +262,74 @@
             h = (g / (1.0 + jnp.exp(-g))) * u
             hid[p, :, pl.ds(pl.multiple_of(s * units, units), units)] = h.astype(jnp.bfloat16)
 
+        @pl.when(packs(p))
+        def _():
+            weight = expert_row(block, z)
+            to = slots(weight)
+            hid[p] = jnp.dot(to.astype(jnp.bfloat16), hid[p],
+                             preferred_element_type=jnp.float32).astype(jnp.bfloat16)
+            wcol[p] = jnp.broadcast_to(
+                jnp.sum(to * weight, axis=1, keepdims=True), (rows, rows))
+
+        @pl.when(jnp.logical_not(packs(p)))
+        def _():
+            wcol[p] = jnp.transpose(jnp.broadcast_to(expert_row(block, z), (rows, rows)))
+
+        @pl.when(jnp.logical_not(end))
+        def _():
+            to = slots(expert_row(block, jnp.where(low, 0, top)))
+            place[p] = jnp.transpose(to).astype(jnp.bfloat16)
+
     def expert_rows(p, q):
         val = jnp.dot(hid[p], dn[:, cols(q)], preferred_element_type=jnp.float32)
         w = wcol[p]
         for b in range(wcols // HB):
             acc[:, b * HB:(b + 1) * HB] = val[:, b * HB:(b + 1) * HB] * w
 
+    def add_in(p, home, q, up):
+        source = from_lo if up else from_hi
+        packed = (z == 1) if up else (z == top - 1)
+
+        @pl.when(packed)
+        def _():
+            ret_copy(home, q, up, cap).wait_recv()
+            acc[...] += jnp.dot(place[p][:, :cap], source[home, :cap, cols(q)],
+                                preferred_element_type=jnp.float32)
+
+        @pl.when(jnp.logical_not(packed))
+        def _():
+            ret_copy(home, q, up, rows).wait_recv()
+            acc[...] += source[home, :, cols(q)].astype(jnp.float32)
+
     def give_back(p, q):
         home = home_of(p)
         expert_rows(p, q)
 
         @pl.when((home > z) & (z > 0))
         def _():
-            ret_copy(home, q, True).wait_recv()
-            acc[...] += from_lo[home, :, cols(q)].astype(jnp.float32)
+            add_in(p, home, q, True)
 
         @pl.when((home < z) & (z < top))
         def _():
-            ret_copy(home, q, False).wait_recv()
-            acc[...] += from_hi[home, :, cols(q)].astype(jnp.float32)
+            add_in(p, home, q, False)
 
         outbox[home, :, cols(q)] = acc[...].astype(jnp.bfloat16)
 
-        @pl.when(home > z)
-        def _():
-            ret_copy(home, q, True).start()
-
-        @pl.when(home < z)
-        def _():
-            ret_copy(home, q, False).start()
+        @pl.when((home > z) & end)
+        def _():
+            ret_copy(home, q, True, cap).start()
+
+        @pl.when((home > z) & jnp.logical_not(end))
+        def _():
+            ret_copy(home, q, True, rows).start()
+
+        @pl.when((home < z) & end)
+        def _():
+            ret_copy(home, q, False, cap).start()
+
+        @pl.when((home < z) & jnp.logical_not(end))
+        def _():
+            ret_copy(home, q, False, rows).start()
 
     wait_weights(0)
     wait_weights(1)
@@ -304,6 +356,10 @@
 
         relay(planes - 1, k)
 
+        @pl.when(jnp.logical_not(end) & ((k == 1) | (k == 4)))
+        def _():
+            make_hidden(jnp.where(k == 1, 3, 2))
+
         @pl.when(k > 1)
         def _():
             first_back(k - 2)
@@ -312,13 +368,25 @@
     first_back(steps - 2)
     first_back(steps - 1)
 
-    @pl.loop(2, planes)
-    def _(p):
-        make_hidden(p)
-
-        @pl.loop(0, steps)
-        def _(q):
-            give_back(p, q)
+    @pl.when(end)
+    def _():
+        make_hidden(2)
+
+    lag = jnp.where(end, steps, 2)
+
+    @pl.loop(0, 2 * steps)
+    def _(i):
+        @pl.when(i < steps)
+        def _():
+            give_back(2, i)
+
+        @pl.when(end & (i == steps))
+        def _():
+            make_hidden(3)
+
+        @pl.when((i >= lag) & (i < lag + steps))
+        def _():
+            give_back(3, i - lag)
 
     make_hidden(0)
 
@@ -328,13 +396,11 @@
 
         @pl.when(z > 0)
         def _():
-            ret_copy(z, q, True).wait_recv()
-            acc[...] += from_lo[z, :, cols(q)].astype(jnp.float32)
+            add_in(0, z, q, True)
 
         @pl.when(z < top)
         def _():
-            ret_copy(z, q, False).wait_recv()
-            acc[...] += from_hi[z, :, cols(q)].astype(jnp.float32)
+            add_in(0, z, q, False)
 
         out_ref[:, cols(q)] = acc[...].astype(jnp.bfloat16)
 
@@ -359,17 +425,19 @@
                 def _(q):
                     tok_copy(block, q, up).wait_send()
 
-        @pl.when(block != z)
-        def _():
-            @pl.loop(0, steps)
-            def _(q):
-                ret_copy(block, q, True).wait_send()
+        for n, mine in ((cap, end), (rows, jnp.logical_not(end))):
+            @pl.when((block != z) & mine)
+            def _():
+                @pl.loop(0, steps)
+                def _(q):
+                    ret_copy(block, q, True, n).wait_send()
 
 
 def on_slice(planes, tokens, routes, gates, gate_weight, up_weight, down_weight):
     rows, width = tokens.shape
     units = gate_weight.shape[1]
     steps = 7
+    capacity = SHARDS * max(1, 3 * rows * routes.shape[1] // (2 * planes * SHARDS))
     lanes = jnp.arange(8, dtype=jnp.int32)[:, None, None]
     wt = jnp.sum(jnp.where(routes[None] == lanes, gates[None], 0.0), axis=2)
     vmem = pl.BlockSpec(memory_space=pltpu.VMEM)
@@ -377,7 +445,7 @@
     dma = pltpu.SemaphoreType.DMA
     bf16, f32 = jnp.bfloat16, jnp.float32
     return pl.pallas_call(
-        functools.partial(layer_kernel, planes, steps),
+        functools.partial(layer_kernel, planes, steps, capacity),
         out_shape=jax.ShapeDtypeStruct((rows, width), bf16),
         in_specs=[vmem] * 3 + [anywhere] * 3,
         out_specs=vmem,
@@ -385,6 +453,7 @@
             pltpu.VMEM((planes, rows, width), bf16),
             pltpu.VMEM((planes, 8, rows), f32),
             pltpu.VMEM((planes, rows, rows), f32),
+            pltpu.VMEM((planes, rows, rows), bf16),
             pltpu.VMEM((SHARDS, 2, width, units), bf16),
             pltpu.VMEM((SHARDS * units, width), bf16),
             pltpu.VMEM((planes, rows, SHARDS * units), bf16),

time: 137 us -> 126 us (0.920)
  Pallas kernels: 133 us -> 121 us
    pallas_call x1, Pallas kernels: 133 us -> 121 us  [on_slice(): pl.pallas_call(functools.partial(layer_kernel, planes, steps, capacity),...]
where the time goes in v3:
time: 126 us
  Pallas kernels  121 us (96%)
  local copies, waits for them, and re-layouts  2.16 us (2%)
  other arithmetic  2.11 us (2%)
    pallas_call x1, Pallas kernels, on_slice(): pl.pallas_call(functools.partial(layer_kernel, planes, steps, capacity),...  121 us

profile of v3, /device:TPU:0, one launch (start us, length us, event | category | flops | bytes accessed | tf_op | source)
XLA Modules:
  0.0 125.6 jit_solution(16807189212886359646)
XLA Ops:
  0.0 1.3 %select_reduce_fusion.wt_ref = f32[8,128]{1,0:T(8,128)} fusion(f32[128,2]{0,1:T(2,128)} %param.8, s32[128,2]{0,1:T(2,128)} %param.7), kind=kLoop, calls=%fused_computation.7 | loop fusion | flops 5120 | bytes 6144 | tf_op jit(solution)/shard_map/reduce_sum | solution.py:442
  1.3 0.8 fusion.3.had_ref
  2.1 121.3 %shard_map.64 = bf16[128,3584]{1,0:T(8,128)(2,1)} custom-call(bf16[128,3584]{1,0:T(8,128)(2,1)} %tok_ref.1, f32[8,128]{1,0:T(8,128)} %select_reduce_fusion.wt_ref, bf16[128,128]{1,0:T(8,128)(2,1)} %fusion.3.had_ref, bf16[3584,256]{1,0:T(8,128)(2,1)} %gate_ref.1, bf16[3584,256]{1,0:T(8,128)(2,1)} %up_ref.1, bf16[256,3584]{1,0:T(8,128)(2,1)} %down_ref.1), custom_call_target="tpu_custom_call" | custom-call | tf_op jit(solution)/shard_map/pallas_call | solution.py:447
  123.5 2.2 %copy.10 = bf16[128,3584]{1,0:T(8,128)(2,1)} copy(bf16[128,3584]{1,0:T(8,128)(2,1)} %shard_map.64) | data formatting | bytes 1835008
  (4 shorter events, 0.0 us)

commit v4 on v3

--- a/solution.py
+++ b/solution.py
@@ -356,7 +356,7 @@
 
         relay(planes - 1, k)
 
-        @pl.when(jnp.logical_not(end) & ((k == 1) | (k == 4)))
+        @pl.when((k == 1) | (jnp.logical_not(end) & (k == 4)))
         def _():
             make_hidden(jnp.where(k == 1, 3, 2))
 
@@ -370,6 +370,8 @@
 
     @pl.when(end)
     def _():
+        give_back(3, 0)
+        give_back(3, 1)
         make_hidden(2)
 
     lag = jnp.where(end, steps, 2)
@@ -380,11 +382,7 @@
         def _():
             give_back(2, i)
 
-        @pl.when(end & (i == steps))
-        def _():
-            make_hidden(3)
-
-        @pl.when((i >= lag) & (i < lag + steps))
+        @pl.when((i >= lag + jnp.where(end, 2, 0)) & (i < lag + steps))
         def _():
             give_back(3, i - lag)
 

time: 126 us -> 128 us (1.016)
  Pallas kernels: 121 us -> 124 us
    pallas_call x1, Pallas kernels: 121 us -> 124 us  [on_slice(): pl.pallas_call(functools.partial(layer_kernel, planes, steps, capacity),...]
where the time goes in v4:
time: 128 us
  Pallas kernels  124 us (97%)
  local copies, waits for them, and re-layouts  2.16 us (2%)
  other arithmetic  2.11 us (2%)
    pallas_call x1, Pallas kernels, on_slice(): pl.pallas_call(functools.partial(layer_kernel, planes, steps, capacity),...  124 us

profile of v4, /device:TPU:0, one launch (start us, length us, event | category | flops | bytes accessed | tf_op | source)
XLA Modules:
  0.0 128.0 jit_solution(4488020591667732559)
XLA Ops:
  0.0 1.3 %select_reduce_fusion.wt_ref = f32[8,128]{1,0:T(8,128)} fusion(f32[128,2]{0,1:T(2,128)} %param.8, s32[128,2]{0,1:T(2,128)} %param.7), kind=kLoop, calls=%fused_computation.7 | loop fusion | flops 5120 | bytes 6144 | tf_op jit(solution)/shard_map/reduce_sum | solution.py:440
  1.3 0.8 fusion.3.had_ref
  2.1 123.7 %shard_map.64 = bf16[128,3584]{1,0:T(8,128)(2,1)} custom-call(bf16[128,3584]{1,0:T(8,128)(2,1)} %tok_ref.1, f32[8,128]{1,0:T(8,128)} %select_reduce_fusion.wt_ref, bf16[128,128]{1,0:T(8,128)(2,1)} %fusion.3.had_ref, bf16[3584,256]{1,0:T(8,128)(2,1)} %gate_ref.1, bf16[3584,256]{1,0:T(8,128)(2,1)} %up_ref.1, bf16[256,3584]{1,0:T(8,128)(2,1)} %down_ref.1), custom_call_target="tpu_custom_call" | custom-call | tf_op jit(solution)/shard_map/pallas_call | solution.py:445
  125.8 2.2 %copy.10 = bf16[128,3584]{1,0:T(8,128)(2,1)} copy(bf16[128,3584]{1,0:T(8,128)(2,1)} %shard_map.64) | data formatting | bytes 1835008
  (4 shorter events, 0.0 us)
